TPU v7x, 128 devices: a whole 4x4x4 slice. The times are simulated.
128 devices in a mesh: fsdp: 32 (over z, y, core), tensor: 4 (over x).
Axes of the slice: x: 4, y: 4, z: 4, core: 2. Of those that a mesh axis runs over, the one named last changes fastest.
Arguments:
- gradient: bfloat16 [4608, 36864], P('fsdp', 'tensor'), may hold values from -8 to 8
- left_basis: bfloat16 [4608, 256], P('fsdp'), may hold values from -6 to 6
- right_basis: bfloat16 [36864, 256], P('tensor'), may hold values from -6 to 6
- left_scale: float32 [256], replicated, may hold values from 2 to 20
- right_scale: float32 [256], replicated, may hold values from 2 to 20
Outputs:
- update: bfloat16 [4608, 36864], P('fsdp', 'tensor')
- left_basis_new: float32 [4608, 256], P('fsdp')
- left_scale_new: float32 [256], replicated
- right_basis_new: float32 [4, 9216, 256], P('tensor', 'fsdp')
- right_scale_new: float32 [256], replicated
All inputs are finite; a program needn't handle non-finite values.
Results may differ from a plain program's by a relative error of at most 0.0095.
Values may be sent and summed in bfloat16 or wider, within the bound.
No kernel may reach another device: no remote copies, remote signals or barrier semaphores. Data moves between devices by JAX's collectives and lax.ppermute only.
A program may use at most 128 MiB of HBM per device.

v0:
```python
import jax
import jax.numpy as jnp
from jax import lax
from jax.sharding import PartitionSpec as P

D = 4608
FF = 36864


decay_rate = 0.9


def tall_product(first, second):
    return lax.dot_general(
        first, second, (((0,), (0,)), ((), ())), preferred_element_type=jnp.float32
    )


def gram_part(rows, count):
    return (
        jnp.dot(rows.T, rows, precision=lax.Precision.HIGHEST, preferred_element_type=jnp.float32)
        / count
    )


def cholesky_basis(rows, gram):
    lower = jnp.linalg.cholesky(gram)
    basis = lax.linalg.triangular_solve(lower, rows, left_side=False, lower=True, transpose_a=True)
    return (basis, jnp.diagonal(lower))


def shards(gradient, left_basis, right_basis, left_scale, right_scale):
    share_rows = right_basis.shape[0] // lax.axis_size("fsdp")
    projected = tall_product(gradient, left_basis)
    image_sum = lax.psum(
        jnp.dot(gradient, right_basis, preferred_element_type=jnp.float32), "tensor"
    )
    back_part = tall_product(gradient, image_sum.astype(jnp.bfloat16))
    proj_full = lax.psum(projected, "fsdp").astype(jnp.bfloat16)
    back_share = lax.psum_scatter(back_part, "fsdp", scatter_dimension=0, tiled=True)
    left_mix = lax.psum(jnp.dot(gradient, proj_full, preferred_element_type=jnp.float32), "tensor")
    left_rows = decay_rate * left_basis.astype(jnp.float32) * left_scale + left_mix / FF
    own_rows = lax.dynamic_slice_in_dim(
        right_basis, lax.axis_index("fsdp") * share_rows, share_rows, 0
    )
    right_rows = decay_rate * own_rows.astype(jnp.float32) * right_scale + back_share / D
    left_gram = gram_part(left_rows, D)
    right_gram = gram_part(right_rows, FF)
    left_gram = lax.psum(left_gram, "fsdp")
    right_gram = lax.psum(right_gram, ("fsdp", "tensor"))
    left_new, left_scale_new = cholesky_basis(left_rows, left_gram)
    right_new, right_scale_new = cholesky_basis(right_rows, right_gram)
    left_damp = (left_scale_new + 1.0) ** (-0.5) - 1.0
    right_damp = (right_scale_new + 1.0) ** (-0.5) - 1.0
    left_cast = left_new.astype(jnp.bfloat16)
    right_full = lax.all_gather(right_new.astype(jnp.bfloat16), "fsdp", axis=0, tiled=True)
    coeff_sum = lax.psum(
        jnp.dot(gradient, right_full, preferred_element_type=jnp.float32), "tensor"
    )
    right_coeff = (coeff_sum * (right_damp / FF)).astype(jnp.bfloat16)
    mixed = gradient.astype(jnp.float32) + lax.dot_general(
        right_coeff, right_full, (((1,), (1,)), ((), ())), preferred_element_type=jnp.float32
    )
    mixed_cast = mixed.astype(jnp.bfloat16)
    coeff_share = lax.psum_scatter(
        tall_product(mixed_cast, left_cast), "fsdp", scatter_dimension=0, tiled=True
    )
    coeff_cast = (coeff_share * (left_damp / D)).astype(jnp.bfloat16)
    coeff_full = lax.all_gather(coeff_cast, "fsdp", axis=0, tiled=True)
    update = mixed + lax.dot_general(
        left_cast, coeff_full, (((1,), (1,)), ((), ())), preferred_element_type=jnp.float32
    )
    return (update.astype(jnp.bfloat16), left_new, left_scale_new, right_new[None], right_scale_new)


def solution(mesh):
    in_specs = (P("fsdp", "tensor"), P("fsdp", None), P("tensor", None), P(), P())
    out_specs = (P("fsdp", "tensor"), P("fsdp", None), P(), P("tensor", "fsdp", None), P())
    return jax.shard_map(shards, mesh=mesh, in_specs=in_specs, out_specs=out_specs, check_vma=False)
```

profile of v0, /device:TPU:1, one launch (start us, length us, event | category | flops | bytes accessed | tf_op | source)
XLA Modules:
  0.0 934.9 jit_solution(8078980261211486671)
XLA Ops:
  7.2 4.1 fusion.34
  11.4 15.5 %all-reduce.13 = bf16[144,256]{1,0:T(8,128)(2,1)S(1)} all-reduce(f32[144,256]{1,0:T(8,128)S(1)} %fusion.34), channel_id=1, replica_groups=mesh['fsdp'=32,'tensor'=4] {'tensor'}, use_global_device_ids=true, to_apply=%region_0.0 | all-reduce | flops 36864 | bytes 221184 | tf_op jit(solution)/shard_map/psum | solution.py:35
  26.9 5.1 convolution_bitcast_fusion
  32.0 9.6 %copy.27 = f32[9216,256]{1,0:T(8,128)} copy(f32[9216,256]{0,1:T(8,128)} %convolution_bitcast_fusion) | data formatting | bytes 18874368
  42.3 98.0 %reduce-scatter.7.cloned.1.call-done = f32[288,256]{1,0:T(8,128)} async-done(((f32[9216,256]{1,0:T(8,128)}), f32[288,256]{1,0:T(8,128)}) %reduce-scatter.7.cloned.1.call-update) | async-done | bytes 294928 | tf_op jit(solution)/shard_map/reduce_scatter | solution.py:40
  140.3 1.0 multiply_add_fusion
  141.3 1.5 convolution_multiply_fusion.1
  143.7 145.2 %all-reduce.8.cloned.1.call-done = f32[256,256]{0,1:T(8,128)} async-done(((f32[256,256]{0,1:T(8,128)}), f32[256,256]{0,1:T(8,128)}) %all-reduce.8.cloned.1.call-update) | async-done | bytes 262160 | tf_op jit(solution)/shard_map/psum | solution.py:50
  288.8 1.1 copy.22
  289.9 1.0 fusion.9
  290.9 11.7 %cholesky.130 = f32[128,128]{1,0:T(8,128)S(1)} custom-call(f32[128,128]{1,0:T(8,128)S(1)} %cholesky.194), custom_call_target="Cholesky" | custom-call | tf_op jit(solution)/shard_map/jit(cholesky)/cholesky | solution.py:27
  303.3 10.4 %custom-call.21 = f32[1,128,128]{1,2,0:T(8,128)} custom-call(f32[1,128,128]{2,1,0:T(8,128)S(1)} %get-tuple-element.55), custom_call_target="InvertDiagBlocksLowerTriangular" | custom-call | tf_op jit(solution)/shard_map/jit(cholesky)/cholesky | solution.py:27
  314.6 1.0 constant_dynamic-update-slice_fusion.3
  315.6 0.9 convolution_subtract_fusion.3
  316.5 12.5 %cholesky.147 = f32[128,128]{1,0:T(8,128)S(1)} custom-call(f32[128,128]{1,0:T(8,128)} %convolution_subtract_fusion.3), custom_call_target="Cholesky" | custom-call | tf_op jit(solution)/shard_map/jit(cholesky)/cholesky | solution.py:27
  331.1 1.0 fusion.11
  333.4 5.7 while.2
  334.5 2.0 bitcast_dynamic-update-slice_fusion.4
  337.1 2.0 bitcast_dynamic-update-slice_fusion.4
  339.8 21.1 %custom-call.14 = f32[2,128,128]{1,2,0:T(8,128)} custom-call(f32[2,128,128]{2,1,0:T(8,128)} %get-tuple-element.13), custom_call_target="InvertDiagBlocksLowerTriangular" | custom-call | tf_op jit(solution)/shard_map/triangular_solve | solution.py:28
  360.9 1.1 fusion.14
  362.0 1.1 convolution_subtract_fusion
  363.2 1.1 fusion.24
  365.1 5.1 fusion.35
  370.2 178.1 %all-reduce.14 = bf16[9216,256]{1,0:T(8,128)(2,1)} all-reduce(f32[9216,256]{1,0:T(8,128)} %fusion.35), channel_id=1, replica_groups=mesh['fsdp'=32,'tensor'=4] {'fsdp'}, use_global_device_ids=true, to_apply=%region_8.10 | all-reduce | flops 2359296 | bytes 14155776 | tf_op jit(solution)/shard_map/psum | solution.py:39
  548.3 3.9 fusion.5
  552.2 3.9 convolution_bitcast_fusion.1
  556.1 2.3 gather_fusion
  558.5 38.1 %all-reduce.12.cloned.1.call-done = (f32[144,256]{1,0:T(8,128)}, f32[144,256]{1,0:T(8,128)}) async-done(((f32[144,256]{1,0:T(8,128)}, f32[144,256]{1,0:T(8,128)}), (f32[144,256]{1,0:T(8,128)}, f32[144,256]{1,0:T(8,128)})) %all-reduce.12.cloned.1.call-update) | async-done | bytes 294928 | tf_op jit(solution)/shard_map/psum | solution.py:57
  596.6 0.9 multiply_add_fusion.1
  597.5 1.4 convolution_multiply_fusion
  599.1 6.5 convolution_add_fusion.1
  605.7 99.1 %all-reduce.10.cloned.1.call-done = f32[256,256]{0,1:T(8,128)} async-done(((f32[256,256]{0,1:T(8,128)}), f32[256,256]{0,1:T(8,128)}) %all-reduce.10.cloned.1.call-update) | async-done | bytes 262160 | tf_op jit(solution)/shard_map/psum | solution.py:49
  704.8 1.1 copy.24
  705.8 1.0 fusion.8
  706.9 11.7 %cholesky.164 = f32[128,128]{1,0:T(8,128)S(1)} custom-call(f32[128,128]{1,0:T(8,128)S(1)} %cholesky.197), custom_call_target="Cholesky" | custom-call | tf_op jit(solution)/shard_map/jit(cholesky)/cholesky | solution.py:27
  719.2 9.8 %custom-call.22 = f32[1,128,128]{1,2,0:T(8,128)S(1)} custom-call(f32[1,128,128]{2,1,0:T(8,128)S(1)} %get-tuple-element.51), custom_call_target="InvertDiagBlocksLowerTriangular" | custom-call | tf_op jit(solution)/shard_map/jit(cholesky)/cholesky | solution.py:27
  729.6 11.7 %cholesky.181 = f32[128,128]{1,0:T(8,128)S(1)} custom-call(f32[128,128]{1,0:T(8,128)S(1)} %convolution_subtract_fusion.2), custom_call_target="Cholesky" | custom-call | tf_op jit(solution)/shard_map/jit(cholesky)/cholesky | solution.py:27
  743.3 4.2 while.3
  744.1 1.4 bitcast_dynamic-update-slice_fusion.5
  746.1 1.4 bitcast_dynamic-update-slice_fusion.5
  747.5 19.7 %custom-call.15 = f32[2,128,128]{1,2,0:T(8,128)S(1)} custom-call(f32[2,128,128]{2,1,0:T(8,128)S(1)} %get-tuple-element.21), custom_call_target="InvertDiagBlocksLowerTriangular" | custom-call | tf_op jit(solution)/shard_map/triangular_solve | solution.py:28
  768.0 7.7 fusion.3
  775.7 2.3 gather_fusion.1
  778.1 91.2 %reduce-scatter.5.cloned.1.call-done = f32[288,256]{1,0:T(8,128)} async-done(((f32[9216,256]{1,0:T(8,128)}), f32[288,256]{1,0:T(8,128)}) %reduce-scatter.5.cloned.1.call-update) | async-done | bytes 294928 | tf_op jit(solution)/shard_map/reduce_scatter | solution.py:65
  869.3 1.6 multiply_convert_fusion
  871.7 49.0 %all-gather.5.cloned.1.call-done = bf16[9216,256]{1,0:T(8,128)(2,1)} async-done(((bf16[288,256]{1,0:T(8,128)(2,1)}), bf16[9216,256]{1,0:T(8,128)(2,1)}) %all-gather.5.cloned.1.call-update) | async-done | bytes 4718608 | tf_op jit(solution)/shard_map/all_gather | solution.py:69
  920.6 7.1 fusion
  (72 shorter events, 12.6 us)
Async XLA Ops:
  7.2 19.7 %copy-start = (bf16[144,9216]{1,0:T(8,128)(2,1)S(1)}, bf16[144,9216]{1,0:T(8,128)(2,1)}, u32[]{:S(2)}) copy-start(bf16[144,9216]{1,0:T(8,128)(2,1)} %param.6) | copy-start | bytes 7962628
  7.2 133.1 %reduce-scatter.7.cloned.1.call-start = ((), (), s32[]{:S(2)}) async-start(), calls=%async_computation.7 | async-start | bytes 9732096 | tf_op jit(solution)/shard_map/reduce_scatter | solution.py:40
  41.6 0.7 copy-start.8
  41.6 323.4 %copy-start.4 = (bf16[144,256]{1,0:T(8,128)(2,1)S(1)}, bf16[144,256]{1,0:T(8,128)(2,1)}, u32[]{:S(2)}) copy-start(bf16[144,256]{1,0:T(8,128)(2,1)} %param.7) | copy-start | bytes 221188
  41.6 247.2 %all-reduce.8.cloned.1.call-start = ((), (), s32[]{:S(2)}) async-start(), calls=%async_computation.2 | async-start | bytes 524288 | tf_op jit(solution)/shard_map/psum | solution.py:50
  142.9 409.3 %all-gather.3.cloned.1.call-start = ((), (), s32[]{:S(2)}) async-start(), calls=%async_computation.3 | async-start | bytes 4866048 | tf_op jit(solution)/shard_map/all_gather | solution.py:56
  302.6 0.6 copy-start.5
  329.1 1.9 copy-start.3
  339.1 0.7 copy-start.1
  365.0 5.2 copy-start.9
  365.0 231.5 %all-reduce.12.cloned.1.call-start = ((), (), s32[]{:S(2)}) async-start(), calls=%async_computation.8 | async-start | bytes 589824 | tf_op jit(solution)/shard_map/psum | solution.py:57
  556.0 148.7 %all-reduce.10.cloned.1.call-start = ((), (), s32[]{:S(2)}) async-start(), calls=%async_computation.4 | async-start | bytes 524288 | tf_op jit(solution)/shard_map/psum | solution.py:49
  558.5 47.2 %copy-start.6 = (f32[256]{0:T(256)}, f32[256]{0:T(256)S(1)}, u32[]{:S(2)}) copy-start(f32[256]{0:T(256)S(1)} %gather_fusion) | copy-start | bytes 3076
  598.9 270.4 %reduce-scatter.5.cloned.1.call-start = ((), (), s32[]{:S(2)}) async-start(), calls=%async_computation.5 | async-start | bytes 9732096 | tf_op jit(solution)/shard_map/reduce_scatter | solution.py:65
  768.0 152.7 %copy-start.2 = (f32[144,256]{1,0:T(8,128)}, f32[144,256]{1,0:T(8,128)S(1)}, u32[]{:S(2)}) copy-start(f32[144,256]{1,0:T(8,128)S(1)} %pad_maximum_fusion.1) | copy-start | bytes 442372
  775.7 145.0 %all-gather.5.cloned.1.call-start = ((), (), s32[]{:S(2)}) async-start(), calls=%async_computation.6 | async-start | bytes 4866048 | tf_op jit(solution)/shard_map/all_gather | solution.py:69
  778.1 149.7 %copy-start.7 = (f32[256]{0:T(256)}, f32[256]{0:T(256)S(1)}, u32[]{:S(2)}) copy-start(f32[256]{0:T(256)S(1)} %gather_fusion.1) | copy-start | bytes 3076
Sparse Core Ops, SparseCore 0:
  41.8 98.4 reduce-scatter.6
  146.3 142.4 all-reduce.7
  365.1 51.7 all-gather.2
  556.2 40.3 all-reduce.11
  600.6 104.1 all-reduce.9
  775.8 93.4 reduce-scatter.4
  872.3 48.2 all-gather.4
where the time goes:
time: 939 us; the launch traced here: 935 us
  waiting for transfers between devices  521 us (55%)
  blocking collectives  194 us (21%)
  other arithmetic  119 us (13%)
  matrix products  52.7 us (6%)
  local copies, waits for them, and re-layouts  29.7 us (3%)
  between operations  17.3 us (2%)
    psum x1, blocking collectives, shards(): proj_full = lax.psum(projected, 'fsdp').astype(jnp.bfloat16)  178 us
    psum x1, waiting for transfers between devices, shards(): right_gram = lax.psum(right_gram, ('fsdp', 'tensor'))  145 us
    psum x1, waiting for transfers between devices, shards(): left_gram = lax.psum(left_gram, 'fsdp')  99.1 us
    reduce_scatter x1, waiting for transfers between devices, shards(): lax.psum_scatter(back_part, 'fsdp', scatter_dimension=0, tiled=True)  98 us
    reduce_scatter x1, waiting for transfers between devices, shards(): lax.psum_scatter(tall_product(mixed_cast, left_cast), 'fsdp', scatter_dim...  91.2 us
    another operation x13, other arithmetic, cholesky_basis(): lower = jnp.linalg.cholesky(gram)  70 us
    all_gather x1, waiting for transfers between devices, shards(): coeff_full = lax.all_gather(coeff_cast, 'fsdp', axis=0, tiled=True)  49 us
    another operation x6, other arithmetic, cholesky_basis(): lax.linalg.triangular_solve(lower, rows, left_side=False, lower=True, tra...  42.3 us
  transfers between devices with their start and end apart: 7, of which 6 were waited for; matrix products, arithmetic and copies ran while one was open for 2% of the time, Pallas kernels for 0%

commit v1 on v0

v1 whole, which is shorter than its diff:
```python
import jax
import jax.numpy as jnp
from jax import lax
from jax.experimental import pallas as pl
from jax.experimental.pallas import tpu as pltpu
from jax.sharding import PartitionSpec as P

D = 4608
FF = 36864
RANK = 256
BLOCK = 64
HIGHEST = lax.Precision.HIGHEST

def eliminate(group_list):
    count = BLOCK // 8
    many = 4
    row_iota = lax.broadcasted_iota(jnp.int32, (8, 2 * BLOCK), 0)
    for j in range(0, BLOCK, many):
        g, s = j // 8, j % 8
        for groups in group_list:
            columns = [
                [jnp.broadcast_to(x[:, j + k : j + k + 1], x.shape) for x in groups[g:]]
                for k in range(many)
            ]
            pivot_rows = [groups[g][s + k : s + k + 1] for k in range(many)]
            inverses = []
            for k in range(many):
                here = columns[k]
                inverse = 1.0 / here[0][s + k : s + k + 1]
                inverses.append(inverse)
                for m in range(k + 1, many):
                    low = columns[m][0][s + k : s + k + 1] * inverse
                    pivot_rows[m] = pivot_rows[m] - low * pivot_rows[k]
                    columns[m] = [x - y * low for x, y in zip(columns[m], here)]
            pivot_rows = [row * inverse for row, inverse in zip(pivot_rows, inverses)]
            for i in range(g, count):
                value = groups[i]
                for k in range(many):
                    part = columns[k][i - g]
                    if i == g:
                        part = jnp.where(row_iota > s + k, part, 0.0)
                    value = value - part * pivot_rows[k]
                groups[i] = value
    return group_list


def factor(works, invs, diags):
    for inv in invs:
        inv[...] = jnp.zeros_like(inv)
    row = lax.broadcasted_iota(jnp.int32, (BLOCK, 2 * BLOCK), 0)
    col = lax.broadcasted_iota(jnp.int32, (BLOCK, 2 * BLOCK), 1)
    unit = jnp.where(col - BLOCK == row, 1.0, 0.0).astype(jnp.float32)
    diag_mask = col == row
    for k in range(0, RANK, BLOCK):
        end = k + BLOCK
        start = []
        for work in works:
            x = jnp.concatenate([work[k:end, k:end], unit[:, BLOCK:]], axis=1)
            start.append([x[i : i + 8] for i in range(0, BLOCK, 8)])
        done = eliminate(start)
        for groups, work, inv, diag in zip(done, works, invs, diags):
            x = jnp.concatenate(groups, axis=0)
            pivots = jnp.sum(jnp.where(diag_mask, x, 0.0), axis=1, keepdims=True)
            x = x * lax.rsqrt(pivots)
            diag[:, k:end] = jnp.sum(jnp.where(diag_mask, x, 0.0), axis=0, keepdims=True)[:, :BLOCK]
            t = x[:, BLOCK:]
            inv[k:end, k:end] = t
            if k:
                inv[k:end, :k] = jnp.dot(t, inv[k:end, :k], precision=HIGHEST, preferred_element_type=jnp.float32)
            if end < RANK:
                u = jnp.dot(t, work[k:end, end:], precision=HIGHEST, preferred_element_type=jnp.float32)
                both = jnp.concatenate([inv[k:end, :end], u], axis=1)
                step = lax.dot_general(u, both, (((0,), (0,)), ((), ())), precision=HIGHEST, preferred_element_type=jnp.float32)
                inv[end:, :end] -= step[:, :end]
                work[end:, end:] -= step[:, end:]


decay_rate = 0.9
ROWS = 144
SHARE = 288
OWN = 36
LINE = 40
FOUR = 4 * LINE
WIDE = 4 * SHARE
PIECE = 16 * LINE
TILES = WIDE // 128
TALL = 328
SIDE = 64 * LINE


def tall_product(first, second):
    return lax.dot_general(
        first, second, (((0,), (0,)), ((), ())), preferred_element_type=jnp.float32
    )


def wide_product(first, second):
    return lax.dot_general(
        first, second, (((1,), (1,)), ((), ())), preferred_element_type=jnp.float32
    )


def times_inverse(rows, inverse):
    return lax.dot_general(
        rows,
        inverse,
        (((1,), (1,)), ((), ())),
        precision=HIGHEST,
        preferred_element_type=jnp.float32,
    )


def whole():
    return pl.BlockSpec(memory_space=pltpu.VMEM)


LIMIT = pltpu.CompilerParams(vmem_limit_bytes=62 * 1024 * 1024)


def stack_tiles(value):
    tiles = [value[:, 128 * k : 128 * (k + 1)] for k in range(TILES)]
    tiles.append(jnp.zeros((TALL - OWN * TILES, 128), jnp.float32))
    return jnp.concatenate(tiles, axis=0).astype(jnp.bfloat16)


def unstack_tiles(value):
    value = value.astype(jnp.float32)
    return jnp.concatenate([value[OWN * k : OWN * (k + 1)] for k in range(TILES)], axis=1)


def pack_kernel(block_ref, out_ref):
    value = block_ref[...].astype(jnp.float32)
    for p in range(8):
        quarters = [
            value[t * OWN : (t + 1) * OWN, p * SHARE : (p + 1) * SHARE] for t in range(4)
        ]
        out_ref[p] = stack_tiles(jnp.concatenate(quarters, axis=1))


def pack(block):
    n_row = FF // 4 // SHARE
    return pl.pallas_call(
        pack_kernel,
        grid=(n_row // 8,),
        in_specs=[pl.BlockSpec((ROWS, 8 * SHARE), lambda i: (0, i))],
        out_specs=pl.BlockSpec((8, TALL, 128), lambda i: (i, 0, 0)),
        out_shape=jax.ShapeDtypeStruct((n_row, TALL, 128), jnp.bfloat16),
        compiler_params=LIMIT,
    )(block)


def unpack_kernel(parcel_ref, out_ref):
    values = [unstack_tiles(parcel_ref[p]) for p in range(8)]
    quarters = [
        jnp.concatenate([value[:, t * SHARE : (t + 1) * SHARE] for value in values], axis=1)
        for t in range(4)
    ]
    out_ref[...] = jnp.concatenate(quarters, axis=0).astype(jnp.bfloat16)


def unpack(parcels):
    n_row = parcels.shape[0]
    return pl.pallas_call(
        unpack_kernel,
        grid=(n_row // 8,),
        in_specs=[pl.BlockSpec((8, TALL, 128), lambda i: (i, 0, 0))],
        out_specs=pl.BlockSpec((ROWS, 8 * SHARE), lambda i: (0, i)),
        out_shape=jax.ShapeDtypeStruct((ROWS, n_row * SHARE), jnp.bfloat16),
        compiler_params=LIMIT,
    )(parcels)


def strip_kernel(where_ref, parcel_ref, own_ref, scale_ref, *refs):
    piece_refs = refs[:10]
    strip_ref, rows_ref, factor_ref, gram_ref, quarter, work = refs[10:]
    step = pl.program_id(0)

    @pl.when(step == 0)
    def _():
        work[...] = jnp.zeros_like(work)

    lines = []
    empty = jnp.zeros((LINE - OWN, WIDE), jnp.float32)
    for p in range(parcel_ref.shape[0]):
        value = jnp.concatenate([unstack_tiles(parcel_ref[p, 0]), empty], axis=0)
        lines += [value[:, t * SHARE : (t + 1) * SHARE] for t in range(4)]
    strip_ref[0] = jnp.concatenate(lines, axis=0).astype(jnp.bfloat16)
    for t in range(4):
        quarter[t] = jnp.concatenate(lines[t::4], axis=0).astype(jnp.bfloat16)

    def add_products(own, right, across, across_next, left):
        opposite = jnp.where(step % 2 == 0, across[...], across_next[...])
        thin = jnp.concatenate([own[...], right[...], opposite, left[...]], axis=0)
        order = [quarter[(where_ref[1] + d) % 4] for d in range(4)]
        work[...] += tall_product(jnp.concatenate(order, axis=0), thin)

    @pl.when(step < 2)
    def _():
        add_products(*piece_refs[:5])

    @pl.when(step >= 2)
    def _():
        add_products(*piece_refs[5:])

    @pl.when(step == pl.num_programs(0) - 1)
    def _():
        right_rows = (
            decay_rate * own_ref[...].astype(jnp.float32) * scale_ref[...] + work[:, RANK:] / D
        )
        rows_ref[...] = right_rows
        factor_ref[:, :RANK] = work[:, :RANK].astype(jnp.bfloat16)
        factor_ref[:, RANK:] = right_rows.astype(jnp.bfloat16)
        gram_ref[...] = (
            lax.dot_general(
                right_rows,
                right_rows,
                (((0,), (0,)), ((), ())),
                precision=HIGHEST,
                preferred_element_type=jnp.float32,
            )
            / FF
        )


def smem():
    return pl.BlockSpec(memory_space=pltpu.SMEM)


def strip_products(where, parcels, own_rows, right_scale, pieces):
    block = 8 * FOUR

    def fixed(shape):
        return pl.BlockSpec(shape, lambda i, where: (0,) * len(shape))

    def by_core(shape):
        return pl.BlockSpec(shape, lambda i, where: (i % 2, (where[0] + i // 2) % 2, 0, 0))

    mine = pl.BlockSpec((8 * LINE, 2 * RANK), lambda i, where: (jnp.minimum(i, 1), 0))
    other = pl.BlockSpec((8 * LINE, 2 * RANK), lambda i, where: (jnp.maximum(i - 2, 0), 0))
    half = fixed((8 * LINE, 2 * RANK))
    return pl.pallas_call(
        strip_kernel,
        grid_spec=pltpu.PrefetchScalarGridSpec(
            num_scalar_prefetch=1,
            grid=(4,),
            in_specs=[
                by_core((8, 1, TALL, 128)),
                fixed((SHARE, RANK)),
                fixed((1, RANK)),
            ]
            + [mine, mine, half, half, mine]
            + [other, other, half, half, other],
            out_specs=(
                pl.BlockSpec((1, block, SHARE), lambda i, where: (i // 2, i % 2, 0)),
                fixed((SHARE, RANK)),
                fixed((SHARE, 2 * RANK)),
                fixed((RANK, RANK)),
            ),
            scratch_shapes=[
                pltpu.VMEM((4, 8 * LINE, SHARE), jnp.bfloat16),
                pltpu.VMEM((SHARE, 2 * RANK), jnp.float32),
            ],
        ),
        out_shape=(
            jax.ShapeDtypeStruct((2, SIDE, SHARE), jnp.bfloat16),
            jax.ShapeDtypeStruct((SHARE, RANK), jnp.float32),
            jax.ShapeDtypeStruct((SHARE, 2 * RANK), jnp.bfloat16),
            jax.ShapeDtypeStruct((RANK, RANK), jnp.float32),
        ),
        compiler_params=LIMIT,
    )(
        where,
        parcels.reshape(16, 2, TALL, 128),
        own_rows,
        right_scale[None],
        *pieces,
    )


def away_kernel(strip_ref, factor_ref, out_ref):
    out_ref[...] = jnp.dot(
        strip_ref[0], factor_ref[...], preferred_element_type=jnp.float32
    ).astype(jnp.bfloat16)


def home_kernel(
    where_ref, strip_ref, factor_ref, other_ref, gram_ref, other_gram_ref, out_ref
):
    step = pl.program_id(0)
    product = jnp.dot(strip_ref[0], factor_ref[...], preferred_element_type=jnp.float32)
    product = product + other_ref[...].astype(jnp.float32)
    rows = pl.ds(pl.multiple_of(where_ref[0] * 128 + step * 32, 32), 32)
    gram = gram_ref[rows] + other_gram_ref[rows]
    high = gram.astype(jnp.bfloat16)
    low = (gram - high.astype(jnp.float32)).astype(jnp.bfloat16)
    to = lax.broadcasted_iota(jnp.int32, (8 * 16, 32), 0)
    source = lax.broadcasted_iota(jnp.int32, (8 * 16, 32), 1)
    spare = to % 8 - (OWN - 32)
    pick = jnp.where(
        (to // 8 * 2 + spare == source) & (spare >= 0) & (spare < 2), 1.0, 0.0
    ).astype(jnp.bfloat16)
    tail = jnp.concatenate(
        [
            jnp.dot(pick, high, preferred_element_type=jnp.float32),
            jnp.dot(pick, low, preferred_element_type=jnp.float32),
        ],
        axis=1,
    )
    lines = []
    for c in range(16):
        line = product[c * LINE : (c + 1) * LINE]
        lines += [line[:32], line[32:] + tail[c * 8 : (c + 1) * 8]]
    out_ref[...] = jnp.concatenate(lines, axis=0).astype(jnp.bfloat16)


def away_sums(strip, factors):
    return pl.pallas_call(
        away_kernel,
        grid=(4,),
        in_specs=[
            pl.BlockSpec((1, PIECE, SHARE), lambda i: (1, i, 0)),
            pl.BlockSpec((SHARE, 2 * RANK), lambda i: (0, 0)),
        ],
        out_specs=pl.BlockSpec((PIECE, 2 * RANK), lambda i: (i, 0)),
        out_shape=jax.ShapeDtypeStruct((SIDE, 2 * RANK), jnp.bfloat16),
        compiler_params=LIMIT,
    )(strip, factors)


def home_sums(where, strip, factors, other, gram, other_gram):
    sums = pl.pallas_call(
        home_kernel,
        grid_spec=pltpu.PrefetchScalarGridSpec(
            num_scalar_prefetch=1,
            grid=(4,),
            in_specs=[
                pl.BlockSpec((1, PIECE, SHARE), lambda i, where: (0, i, 0)),
                pl.BlockSpec((SHARE, 2 * RANK), lambda i, where: (0, 0)),
                pl.BlockSpec((PIECE, 2 * RANK), lambda i, where: (i, 0)),
                pl.BlockSpec((RANK, RANK), lambda i, where: (0, 0)),
                pl.BlockSpec((RANK, RANK), lambda i, where: (0, 0)),
            ],
            out_specs=pl.BlockSpec((PIECE, 2 * RANK), lambda i, where: (i, 0)),
        ),
        out_shape=jax.ShapeDtypeStruct((SIDE, 2 * RANK), jnp.bfloat16),
        compiler_params=LIMIT,
    )(where, strip, factors, other, gram, other_gram)
    return sums.reshape(64, LINE, 2 * RANK)


def lines_kernel(sums_ref, basis_ref, scale_ref, rows_ref, lines_ref, work):
    step = pl.program_id(0)

    @pl.when(step == 0)
    def _():
        work[...] = jnp.zeros_like(work)

    total = work[...]
    for c in range(sums_ref.shape[0]):
        total += sums_ref[c].astype(jnp.float32)
    work[...] = total

    @pl.when(step == pl.num_programs(0) - 1)
    def _():
        left = work[:, :RANK]
        rows = decay_rate * basis_ref[...].astype(jnp.float32) * scale_ref[...] + left / FF
        rows_ref[:, :RANK] = rows
        rows_ref[:, RANK:] = work[:, RANK:]
        gram = left[32:] + work[32:, RANK:]
        high = gram.astype(jnp.bfloat16).astype(jnp.float32)
        low = pltpu.roll(gram - high, 2, 0)
        place = lax.broadcasted_iota(jnp.int32, (8, RANK), 0)
        last = jnp.where(
            place < OWN - 32, rows[32:], jnp.where(place < OWN - 30, high, low)
        )
        line = jnp.concatenate([rows[:32], last], axis=0).astype(jnp.bfloat16)
        lines_ref[...] = jnp.broadcast_to(line[None], lines_ref.shape)


def own_lines(sums, basis, scale):
    per = 16

    def fixed(shape):
        return pl.BlockSpec(shape, lambda i: (0,) * len(shape))

    return pl.pallas_call(
        lines_kernel,
        grid=(sums.shape[0] // per,),
        in_specs=[
            pl.BlockSpec((per, LINE, 2 * RANK), lambda i: (i, 0, 0)),
            fixed((LINE, RANK)),
            fixed((1, RANK)),
        ],
        out_specs=(fixed((LINE, 2 * RANK)), fixed((64, LINE, RANK))),
        out_shape=(
            jax.ShapeDtypeStruct((LINE, 2 * RANK), jnp.float32),
            jax.ShapeDtypeStruct((64, LINE, RANK), jnp.bfloat16),
        ),
        scratch_shapes=[pltpu.VMEM((LINE, 2 * RANK), jnp.float32)],
        compiler_params=LIMIT,
    )(sums, basis, scale[None])


def read_side(lines_ref, left_ref, gram, store):
    valid = lax.broadcasted_iota(jnp.int32, (PIECE, RANK), 0) % LINE < OWN
    to = lax.broadcasted_iota(jnp.int32, (32, PIECE), 0)
    source = lax.broadcasted_iota(jnp.int32, (32, PIECE), 1) - (to // 2 * LINE + OWN + to % 2)
    pick = jnp.where((source == 0) | (source == 2), 1.0, 0.0).astype(jnp.bfloat16)
    gram[...] = jnp.zeros_like(gram)
    for i in range(SIDE // PIECE):
        value = lines_ref[i * PIECE : (i + 1) * PIECE]
        store(i * 32, jnp.dot(pick, value, preferred_element_type=jnp.float32))
        value = jnp.where(valid, value.astype(jnp.float32), 0.0).astype(jnp.bfloat16)
        left_ref[i * PIECE : (i + 1) * PIECE] = value
        gram[...] += tall_product(value, value)


def side_kernel(lines_ref, left_ref, gram_ref, rows_ref):
    def store(spot, value):
        rows_ref[spot : spot + 32] = value

    read_side(lines_ref, left_ref, gram_ref, store)


def own_side(lines):
    return pl.pallas_call(
        side_kernel,
        in_specs=[whole()],
        out_specs=(whole(),) * 3,
        out_shape=(
            jax.ShapeDtypeStruct((SIDE, RANK), jnp.bfloat16),
            jax.ShapeDtypeStruct((RANK, RANK), jnp.float32),
            jax.ShapeDtypeStruct((128, RANK), jnp.float32),
        ),
        compiler_params=LIMIT,
    )(lines)


def factor_kernel(
    where_ref, gram_ref, rows_ref, other_ref, sums_ref, left_ref, coeff_ref, left_inv, right_inv,
    left_diag, right_diag, left_work, right_work,
):
    core = where_ref[0]

    def store(spot, value):
        right_work[pl.ds(pl.multiple_of((1 - core) * 128 + spot, 32), 32)] = value

    read_side(other_ref, left_ref, left_work, store)
    right_work[pl.ds(pl.multiple_of(core * 128, 128), 128)] = rows_ref[...]
    left_work[...] = (gram_ref[...] + left_work[...]) / D
    factor((left_work, right_work), (left_inv, right_inv), (left_diag, right_diag))
    damp = lax.rsqrt(right_diag[...] + 1.0) - 1.0
    coeff = times_inverse(sums_ref[:, RANK:], right_inv[...]) * (damp / FF)
    keep = lax.broadcasted_iota(jnp.int32, (LINE, RANK), 0) < OWN
    coeff = jnp.where(keep, coeff, 0.0).astype(jnp.bfloat16)
    coeff_ref[...] = jnp.broadcast_to(coeff[None], coeff_ref.shape)


def factor_grams(where, gram, rows, other, sums):
    square = jax.ShapeDtypeStruct((RANK, RANK), jnp.float32)
    line = jax.ShapeDtypeStruct((1, RANK), jnp.float32)
    return pl.pallas_call(
        factor_kernel,
        in_specs=[smem()] + [whole()] * 4,
        out_specs=(whole(),) * 6,
        out_shape=(
            jax.ShapeDtypeStruct((SIDE, RANK), jnp.bfloat16),
            jax.ShapeDtypeStruct((64, LINE, RANK), jnp.bfloat16),
            square,
            square,
            line,
            line,
        ),
        scratch_shapes=[pltpu.VMEM((RANK, RANK), jnp.float32)] * 2,
        compiler_params=LIMIT,
    )(where, gram, rows, other, sums)


def mix(strip, coeff, new, left, work):
    value = strip.astype(jnp.float32) + wide_product(coeff, new.astype(jnp.bfloat16))
    work[...] += tall_product(value.astype(jnp.bfloat16), left)
    return value


def mixed_kernel(strip_ref, coeff_ref, left_ref, new_ref, mixed_ref, work_ref):
    @pl.when(pl.program_id(0) == 0)
    def _():
        work_ref[...] = jnp.zeros_like(work_ref)

    mixed_ref[...] = mix(strip_ref[0], coeff_ref[...], new_ref[...], left_ref[...], work_ref)


def own_mixed(strip, mine, left_mine, right_new):
    block = 8 * FOUR
    part = pl.BlockSpec((block, RANK), lambda i: (i, 0))
    fixed = pl.BlockSpec((SHARE, RANK), lambda i: (0, 0))
    return pl.pallas_call(
        mixed_kernel,
        grid=(2,),
        in_specs=[pl.BlockSpec((1, block, SHARE), lambda i: (0, i, 0)), part, part, fixed],
        out_specs=(pl.BlockSpec((block, SHARE), lambda i: (i, 0)), fixed),
        out_shape=(
            jax.ShapeDtypeStruct((SIDE, SHARE), jnp.float32),
            jax.ShapeDtypeStruct((SHARE, RANK), jnp.float32),
        ),
        compiler_params=LIMIT,
    )(strip, mine, left_mine, right_new)


def update_kernel(
    where_ref, strip_ref, coeff_ref, mixed_ref, work_ref, left_mine, left_other, new_ref,
    damp_ref, out_ref, mixed, work, left_coeff,
):
    step = pl.program_id(0)
    block = strip_ref.shape[1]

    def spot(index):
        return pl.ds(pl.multiple_of(index * block, block), block)

    @pl.when(step == 0)
    def _():
        work[...] = work_ref[...]

    @pl.when(step < 2)
    def _():
        mixed[spot(step)] = mix(
            strip_ref[0], coeff_ref[...], new_ref[...], left_other[spot(step)], work
        )

    @pl.when(step == 2)
    def _():
        left_coeff[...] = (work[...] * (damp_ref[...] / D)).astype(jnp.bfloat16)

    def write(value, left):
        value = value + wide_product(left, left_coeff[...])
        for p in range(block // FOUR):
            quarters = [
                value[p * FOUR + t * LINE : p * FOUR + t * LINE + OWN] for t in range(4)
            ]
            out_ref[p, 0] = stack_tiles(jnp.concatenate(quarters, axis=1))

    @pl.when((step >= 2) & (step < 4))
    def _():
        write(mixed_ref[...], left_mine[spot(step - 2)])

    @pl.when(step >= 4)
    def _():
        write(mixed[spot(step - 4)], left_other[spot(step - 4)])


def update_parcels(where, strip, other, mixed, work, left_mine, left_other, right_new, left_damp):
    block = 8 * FOUR

    def fixed(shape):
        return pl.BlockSpec(shape, lambda i, where: (0,) * len(shape))

    def out_block(i, where):
        place = jnp.maximum(i - 2, 0)
        return (place % 2, (where[0] + place // 2) % 2, 0, 0)

    parcels = pl.pallas_call(
        update_kernel,
        grid_spec=pltpu.PrefetchScalarGridSpec(
            num_scalar_prefetch=1,
            grid=(6,),
            in_specs=[
                pl.BlockSpec((1, block, SHARE), lambda i, where: (1, jnp.minimum(i, 1), 0)),
                pl.BlockSpec((block, RANK), lambda i, where: (jnp.minimum(i, 1), 0)),
                pl.BlockSpec((block, SHARE), lambda i, where: (jnp.clip(i - 2, 0, 1), 0)),
                fixed((SHARE, RANK)),
                fixed((SIDE, RANK)),
                fixed((SIDE, RANK)),
                fixed((SHARE, RANK)),
                fixed((1, RANK)),
            ],
            out_specs=pl.BlockSpec((8, 1, TALL, 128), out_block),
            scratch_shapes=[
                pltpu.VMEM((SIDE, SHARE), jnp.float32),
                pltpu.VMEM((SHARE, RANK), jnp.float32),
                pltpu.VMEM((SHARE, RANK), jnp.bfloat16),
            ],
        ),
        out_shape=jax.ShapeDtypeStruct((16, 2, TALL, 128), jnp.bfloat16),
        compiler_params=LIMIT,
    )(where, strip, other, mixed, work, left_mine, left_other, right_new, left_damp[None])
    return parcels.reshape(32, TALL, 128)


def ring(value, axis):
    found = [value]
    for step in (3, 2, 1):
        found.append(lax.ppermute(value, axis, [(i, (i + step) % 4) for i in range(4)]))
    return found


def swap(value):
    return lax.ppermute(value, "core", [(0, 1), (1, 0)])


def shift(value, step):
    return lax.ppermute(value, "tensor", [(i, (i + step) % 4) for i in range(4)])


def gather_rest(lines):
    left, right = shift(lines, 1), shift(lines, -1)
    half = lines.shape[0] // 2
    mine = [lines, right, shift(left[:half], 1), shift(right[half:], -1), left]
    return mine + [swap(piece) for piece in mine]


def gather_sets(copies, beside=()):
    mine = lax.all_to_all(copies, ("z", "y", "tensor"), 0, 0)
    mine = mine.reshape(SIDE, mine.shape[2])
    mine, beside = lax.optimization_barrier((mine, beside))
    return mine, swap(mine), beside


def image_kernel(spot_ref, basis_ref, first, second, third, fourth, out_ref):
    spot = spot_ref[0]
    image = (first[spot] + second[spot]) + (third[spot] + fourth[spot])
    line = jnp.concatenate([basis_ref[...], image.astype(jnp.bfloat16)], axis=1)
    out_ref[...] = jnp.broadcast_to(line[None], out_ref.shape)


def image_lines(basis, image, packed):
    spot = jnp.reshape(lax.axis_index("tensor"), (1,)).astype(jnp.int32)
    found, packed = lax.optimization_barrier((ring(image, "tensor"), packed))
    copies = pl.pallas_call(
        image_kernel,
        in_specs=[smem()] + [whole()] * 5,
        out_specs=whole(),
        out_shape=jax.ShapeDtypeStruct((16, LINE, 2 * RANK), jnp.bfloat16),
    )(spot, basis, *found)
    lines = lax.all_to_all(copies, ("z", "y"), 0, 0)
    return lines.reshape(PIECE, 2 * RANK), packed


def in_lines(rows):
    return jnp.pad(rows.reshape(4, OWN, RANK), ((0, 0), (0, LINE - OWN), (0, 0)))


def shards(gradient, left_basis, right_basis, left_scale, right_scale):
    t_place = lax.axis_index("tensor")
    place = (lax.axis_index("z") * 4 + lax.axis_index("y")) * 2 + lax.axis_index("core")
    where = jnp.stack([lax.axis_index("core"), t_place]).astype(jnp.int32)
    own_basis = lax.dynamic_slice_in_dim(in_lines(left_basis), t_place, 1, 0)[0]
    own_rows = lax.dynamic_slice_in_dim(right_basis, place * SHARE, SHARE, 0)
    image = jnp.dot(gradient, right_basis, preferred_element_type=jnp.float32)
    thin, packed = image_lines(own_basis, in_lines(image), pack(gradient))
    packed, thin = lax.optimization_barrier((packed, thin))
    parcels = lax.all_to_all(packed, ("z", "y", "core"), 0, 0)
    strip, right_rows, factors, gram = strip_products(
        where, parcels, own_rows, right_scale, gather_rest(thin)
    )
    other = swap(away_sums(strip, factors))
    sums = home_sums(where, strip, factors, other, gram, swap(gram))
    sums = lax.all_to_all(sums, ("z", "y", "tensor"), 0, 0)
    rows, lines = own_lines(sums, own_basis, left_scale)
    mine, other, _ = gather_sets(lines)
    left_mine, left_gram, right_part = own_side(mine)
    left_other, right_coeff, left_inv, right_inv, left_scale_new, right_scale_new = factor_grams(
        where, left_gram, right_part, other, rows
    )
    left_scale_new, right_scale_new = left_scale_new[0], right_scale_new[0]
    left_damp = (left_scale_new + 1.0) ** (-0.5) - 1.0
    left_mine = times_inverse(left_mine.astype(jnp.float32), left_inv).astype(jnp.bfloat16)
    left_other = times_inverse(left_other.astype(jnp.float32), left_inv).astype(jnp.bfloat16)
    right_new = times_inverse(right_rows, right_inv)
    mine, other, (left_mine, left_other, right_new) = gather_sets(
        right_coeff, (left_mine, left_other, right_new)
    )
    mixed, work = own_mixed(strip, mine, left_mine, right_new)
    update = update_parcels(
        where, strip, other, mixed, work, left_mine, left_other, right_new, left_damp
    )
    left_new = times_inverse(rows[:OWN, :RANK], left_inv)
    left_new, update = lax.optimization_barrier((left_new, update))
    left_new = lax.all_gather(left_new, "tensor", axis=0, tiled=True)
    update = unpack(lax.all_to_all(update, ("z", "y", "core"), 0, 0))
    return (update, left_new, left_scale_new, right_new[None], right_scale_new)


def solution(mesh):
    rows = ("z", "y", "core")
    mesh = jax.sharding.Mesh(mesh.devices.reshape(4, 4, 2, 4), rows + ("tensor",))
    in_specs = (P(rows, "tensor"), P(rows, None), P("tensor", None), P(), P())
    out_specs = (P(rows, "tensor"), P(rows, None), P(), P("tensor", rows, None), P())
    return jax.shard_map(shards, mesh=mesh, in_specs=in_specs, out_specs=out_specs, check_vma=False)
```

time: 939 us -> 294 us (0.31)
  waiting for transfers between devices: 521 us -> 62.2 us
  other arithmetic: 119 us -> 1.17 us
  blocking collectives: 194 us -> 97.3 us
  Pallas kernels: 0 us -> 72.1 us
  matrix products: 52.7 us -> 11.2 us
  starting transfers between devices: 0.75 us -> 41.5 us
  local copies, waits for them, and re-layouts: 29.7 us -> 4.8 us
  between operations: 17.3 us -> 0.84 us
    psum x3 -> x0, waiting for transfers between devices: 282 us -> none  [the longest x1 145 us: shards(): right_gram = lax.psum(right_gram, ('fsdp', 'tensor'))]
    psum x2 -> x0, blocking collectives: 194 us -> none  [the longest x1 178 us: shards(): proj_full = lax.psum(projected, 'fsdp').astype(jnp.bfloat16)]
    reduce_scatter x2 -> x0, waiting for transfers between devices: 189 us -> none  [the longest x1 98 us: shards(): lax.psum_scatter(back_part, 'fsdp', scatter_dimension=0, tiled=True)]
    another operation x19 -> x1, other arithmetic: 112 us -> 0.6 us  [shards(): where = jnp.stack([lax.axis_index('core'), t_place]).astype(jnp.int32)]
    all_to_all x0 -> x3, blocking collectives: none -> 86.9 us  [the longest x1 41.6 us: shards(): sums = lax.all_to_all(sums, ('z', 'y', 'tensor'), 0, 0)]
    pallas_call x0 -> x11, Pallas kernels: none -> 72.1 us  [the longest x1 17.1 us: factor_grams(): pl.pallas_call(factor_kernel, in_specs=[smem()] + [whole()] * 4, out_spec...]
    all_gather x2 -> x0, waiting for transfers between devices: 49 us -> none  [the longest x1 49 us: shards(): coeff_full = lax.all_gather(coeff_cast, 'fsdp', axis=0, tiled=True)]
    all_to_all x0 -> x3, waiting for transfers between devices: none -> 37.8 us  [the longest x1 23.2 us: shards(): update = unpack(lax.all_to_all(update, ('z', 'y', 'core'), 0, 0))]
  transfers between devices with their start and end apart: 7 -> 19, of which waited for: 6 -> 8; matrix products, arithmetic and copies ran while one was open for 2% -> 4% of each run, Pallas kernels for 0% -> 4%
where the time goes in v1:
time: 294 us; the launch traced here: 291 us
  blocking collectives  97.3 us (33%)
  Pallas kernels  72.1 us (25%)
  waiting for transfers between devices  62.2 us (21%)
  starting transfers between devices  41.5 us (14%)
  matrix products  11.2 us (4%)
  local copies, waits for them, and re-layouts  4.8 us (2%)
    all_to_all x1, blocking collectives, shards(): sums = lax.all_to_all(sums, ('z', 'y', 'tensor'), 0, 0)  41.6 us
    all_to_all x1, blocking collectives, gather_sets(): mine = lax.all_to_all(copies, ('z', 'y', 'tensor'), 0, 0)  26.3 us
    all_to_all x1, waiting for transfers between devices, shards(): update = unpack(lax.all_to_all(update, ('z', 'y', 'core'), 0, 0))  23.2 us
    all_to_all x1, blocking collectives, image_lines(): lines = lax.all_to_all(copies, ('z', 'y'), 0, 0)  19 us
    ppermute x4, waiting for transfers between devices, shift(): lax.ppermute(value, 'tensor', [(i, (i + step) % 4) for i in range(4)])  18.4 us
    pallas_call x1, Pallas kernels, factor_grams(): pl.pallas_call(factor_kernel, in_specs=[smem()] + [whole()] * 4, out_spec...  17.1 us
    ppermute x9, starting transfers between devices, swap(): return lax.ppermute(value, 'core', [(0, 1), (1, 0)])  13.5 us
    all_to_all x1, waiting for transfers between devices, gather_sets(): mine = lax.all_to_all(copies, ('z', 'y', 'tensor'), 0, 0)  12.7 us
  transfers between devices with their start and end apart: 19, of which 8 were waited for; matrix products, arithmetic and copies ran while one was open for 4% of the time, Pallas kernels for 4%

profile of v1, /device:TPU:1, one launch (start us, length us, event | category | flops | bytes accessed | tf_op | source)
XLA Modules:
  0.0 291.2 jit_solution(10409410934880603656)
XLA Ops:
  0.6 4.0 %fusion.3 = f32[144,256]{1,0:T(8,128)S(1)} fusion(bf16[144,9216]{1,0:T(8,128)(2,1)} %block_ref.1, bf16[9216,256]{1,0:T(8,128)(2,1)} %param.7), kind=kOutput, calls=%fused_computation.9 | convolution fusion | flops 679477248 | bytes 7520256 | tf_op jit(solution)/shard_map/dot_general | solution.py:648
  4.7 2.1 collective-permute-start.2
  6.8 2.5 collective-permute-start.1
  9.3 1.2 collective-permute-start
  10.4 4.5 %shard_map.92 = bf16[32,328,128]{2,1,0:T(8,128)(2,1)} custom-call(bf16[144,9216]{1,0:T(8,128)(2,1)} %block_ref.1), custom_call_target="tpu_custom_call" | custom-call | tf_op jit(solution)/shard_map/pallas_call | solution.py:142
  15.0 0.6 fusion.2.basis_ref
  15.6 0.8 collective-permute-done.1.third
  16.4 0.6 copy-done.16
  17.1 2.0 shard_map.93
  19.2 19.0 %all_to_all.30 = bf16[16,40,512]{2,1,0:T(8,128)(2,1)S(1)} all-to-all(bf16[16,40,512]{2,1,0:T(8,128)(2,1)} %shard_map.93), channel_id=1, replica_groups=mesh['z'=4,'y'=4,'core'=2,'tensor'=4] {'z','y'}, dimensions={0} | all-to-all | bytes 1310720 | tf_op jit(solution)/shard_map/all_to_all | solution.py:634
  38.2 7.1 %all-to-all-start.1 = ((bf16[32,328,128]{2,1,0:T(8,128)(2,1)}), bf16[32,328,128]{2,1,0:T(8,128)(2,1)}, u32[]{:S(2)}, u32[]{:S(2)}) async-start(bf16[32,328,128]{2,1,0:T(8,128)(2,1)} %shard_map.92), calls=%async_computation.1 | async-start | bytes 5373952 | tf_op jit(solution)/shard_map/all_to_all | solution.py:651
  45.3 1.3 collective-permute-start.4
  46.6 1.4 collective-permute-start.3
  48.0 1.0 collective-permute-start.7
  49.0 13.6 %collective-permute-done.4.refs_4_ = bf16[640,512]{1,0:T(8,128)(2,1)S(1)} collective-permute-done((bf16[640,512]{1,0:T(8,128)(2,1)S(1)}, bf16[640,512]{1,0:T(8,128)(2,1)S(1)}, u32[]{:S(2)}, u32[]{:S(2)}) %collective-permute-start.4) | collective-permute-done | bytes 655392 | tf_op jit(solution)/shard_map/ppermute | solution.py:601
  62.7 1.4 collective-permute-start.11
  64.2 2.7 collective-permute-start.6
  67.1 4.9 %collective-permute-done.5.refs_2_ = bf16[320,512]{1,0:T(8,128)(2,1)} collective-permute-done((bf16[320,512]{1,0:T(8,128)(2,1)S(1)}, bf16[320,512]{1,0:T(8,128)(2,1)}, u32[]{:S(2)}, u32[]{:S(2)}) %collective-permute-start.5) | collective-permute-done | bytes 327712 | tf_op jit(solution)/shard_map/ppermute | solution.py:601
  72.0 2.1 collective-permute-start.9
  74.1 0.7 collective-permute-start.10
  74.8 0.6 pad_add_fusion.where_ref
  75.4 1.6 constant_dynamic-slice_fusion.own_ref
  77.0 0.8 copy-done.8
  77.8 1.8 all-to-all-done.1
  79.6 10.1 %shard_map.94 = (bf16[2,2560,288]{2,1,0:T(8,128)(2,1)}, f32[288,256]{1,0:T(8,128)}, bf16[288,512]{1,0:T(8,128)(2,1)}, f32[256,256]{1,0:T(8,128)}) custom-call(s32[2]{0:T(128)} %pad_add_fusion.where_ref, bf16[16,2,328,128]{3,2,1,0:T(8,128)(2,1)} %bitcast.4.parcel_ref, bf16[288,256]{1,0:T(8,128)(2,1)} %constant_dynamic-slice_fusion.own_ref, ...), custom_call_target="tpu_custom_call" | custom-call | tf_op jit(solution)/shard_map/pallas_call | solution.py:241
  89.7 4.9 %shard_map.95 = bf16[2560,512]{1,0:T(8,128)(2,1)} custom-call(bf16[2,2560,288]{2,1,0:T(8,128)(2,1)} %get-tuple-element.42.strip_ref, bf16[288,512]{1,0:T(8,128)(2,1)} %get-tuple-element.43.factor_ref), custom_call_target="tpu_custom_call" | custom-call | tf_op jit(solution)/shard_map/pallas_call | solution.py:317
  94.6 2.8 collective-permute-start.12
  97.5 4.7 %collective-permute-done.13.other_gram_ref = f32[256,256]{1,0:T(8,128)S(1)} collective-permute-done((f32[256,256]{1,0:T(8,128)S(1)}, f32[256,256]{1,0:T(8,128)S(1)}, u32[]{:S(2)}, u32[]{:S(2)}) %collective-permute-start.13) | collective-permute-done | bytes 262176 | tf_op jit(solution)/shard_map/ppermute | solution.py:597
  102.9 6.2 %shard_map.96 = bf16[2560,512]{1,0:T(8,128)(2,1)} custom-call(s32[2]{0:T(128)} %pad_add_fusion.where_ref, bf16[2,2560,288]{2,1,0:T(8,128)(2,1)} %get-tuple-element.42.strip_ref, bf16[288,512]{1,0:T(8,128)(2,1)} %get-tuple-element.43.factor_ref, bf16[2560,512]{1,0:T(8,128)(2,1)} %collective-permute-done.12.other_ref, f32[256,256]{1,0:T(8,128)} %get-tuple-element.44.gram_ref, ...), custom_call_target="tpu_custom_call" | custom-call | tf_op jit(solution)/shard_map/pallas_call | solution.py:331
  109.1 41.6 %all_to_all.31.sums_ref = bf16[64,40,512]{2,1,0:T(8,128)(2,1)} all-to-all(bf16[64,40,512]{2,1,0:T(8,128)(2,1)} %bitcast.26), channel_id=1, replica_groups=mesh['z'=4,'y'=4,'core'=2,'tensor'=4] {'z','y','tensor'}, dimensions={0} | all-to-all | bytes 5242880 | tf_op jit(solution)/shard_map/all_to_all | solution.py:657
  150.7 3.8 %shard_map.97 = (f32[40,512]{1,0:T(8,128)}, bf16[64,40,256]{2,1,0:T(8,128)(2,1)}) custom-call(bf16[64,40,512]{2,1,0:T(8,128)(2,1)} %all_to_all.31.sums_ref, bf16[40,256]{1,0:T(8,128)(2,1)} %fusion.2.basis_ref, f32[1,256]{1,0:T(1,128)} %bitcast.38), custom_call_target="tpu_custom_call" | custom-call | tf_op jit(solution)/shard_map/pallas_call | solution.py:386
  154.6 26.3 %all_to_all.32 = bf16[64,40,256]{2,1,0:T(8,128)(2,1)S(1)} all-to-all(bf16[64,40,256]{2,1,0:T(8,128)(2,1)} %get-tuple-element.46), channel_id=1, replica_groups=mesh['z'=4,'y'=4,'core'=2,'tensor'=4] {'z','y','tensor'}, dimensions={0} | all-to-all | bytes 2621440 | tf_op jit(solution)/shard_map/all_to_all | solution.py:612
  180.9 2.4 collective-permute-start.14
  183.3 3.2 %shard_map.98 = (bf16[2560,256]{1,0:T(8,128)(2,1)}, f32[256,256]{1,0:T(8,128)}, f32[128,256]{1,0:T(8,128)}) custom-call(bf16[2560,256]{1,0:T(8,128)(2,1)} %bitcast.28), custom_call_target="tpu_custom_call" | custom-call | tf_op jit(solution)/shard_map/pallas_call | solution.py:426
  186.5 17.1 %shard_map.99 = (bf16[2560,256]{1,0:T(8,128)(2,1)}, bf16[64,40,256]{2,1,0:T(8,128)(2,1)}, f32[256,256]{1,0:T(8,128)}, f32[256,256]{1,0:T(8,128)}, f32[1,256]{1,0:T(1,128)}, /*index=5*/f32[1,256]{1,0:T(1,128)}) custom-call(s32[2]{0:T(128)} %pad_add_fusion.where_ref, f32[256,256]{1,0:T(8,128)} %get-tuple-element.47.gram_ref, ...), custom_call_target="tpu_custom_call" | custom-call | tf_op jit(solution)/shard_map/pallas_call | solution.py:462
  203.7 5.1 %all-to-all-start.4 = ((bf16[64,40,256]{2,1,0:T(8,128)(2,1)}), bf16[64,40,256]{2,1,0:T(8,128)(2,1)S(1)}, u32[]{:S(2)}, u32[]{:S(2)}) async-start(bf16[64,40,256]{2,1,0:T(8,128)(2,1)} %get-tuple-element.50), calls=%async_computation.4 | async-start | bytes 2621440 | tf_op jit(solution)/shard_map/all_to_all | solution.py:612
  208.8 2.2 fusion.4.new_ref
  211.0 2.3 convolution_convert_fusion.1.left_ref.left_mine
  213.3 2.4 convolution_convert_fusion.left_other
  215.6 12.7 %all-to-all-done.4 = bf16[64,40,256]{2,1,0:T(8,128)(2,1)S(1)} async-done(((bf16[64,40,256]{2,1,0:T(8,128)(2,1)}), bf16[64,40,256]{2,1,0:T(8,128)(2,1)S(1)}, u32[]{:S(2)}, u32[]{:S(2)}) %all-to-all-start.4) | async-done | bytes 1310752 | tf_op jit(solution)/shard_map/all_to_all | solution.py:612
  228.4 2.8 collective-permute-start.15
  232.1 5.1 %shard_map.100 = (f32[2560,288]{1,0:T(8,128)}, f32[288,256]{1,0:T(8,128)}) custom-call(bf16[2,2560,288]{2,1,0:T(8,128)(2,1)} %get-tuple-element.42.strip_ref, bf16[2560,256]{1,0:T(8,128)(2,1)} %bitcast.30, bf16[2560,256]{1,0:T(8,128)(2,1)} %convolution_convert_fusion.1.left_ref.left_mine, f32[288,256]{1,0:T(8,128)} %fusion.4.new_ref), custom_call_target="tpu_custom_call" | custom-call | tf_op jit(solution)/shard_map/pallas_call | solution.py:497
  237.2 10.6 %shard_map.101 = bf16[16,2,328,128]{3,2,1,0:T(8,128)(2,1)} custom-call(s32[2]{0:T(128)} %pad_add_fusion.where_ref, bf16[2,2560,288]{2,1,0:T(8,128)(2,1)} %get-tuple-element.42.strip_ref, bf16[2560,256]{1,0:T(8,128)(2,1)} %collective-permute-done.15.coeff_ref, f32[2560,288]{1,0:T(8,128)} %get-tuple-element.58.mixed_ref, ...), custom_call_target="tpu_custom_call" | custom-call | tf_op jit(solution)/shard_map/pallas_call | solution.py:561
  247.8 4.6 %all-to-all-start.5 = ((bf16[32,328,128]{2,1,0:T(8,128)(2,1)}), bf16[32,328,128]{2,1,0:T(8,128)(2,1)}, u32[]{:S(2)}, u32[]{:S(2)}) async-start(bf16[32,328,128]{2,1,0:T(8,128)(2,1)} %bitcast.25), calls=%async_computation.5 | async-start | bytes 5373952 | tf_op jit(solution)/shard_map/all_to_all | solution.py:679
  252.4 10.4 %all-gather = f32[4,36,256]{2,1,0:T(8,128)S(1)} all-gather(f32[1,36,256]{2,1,0:T(8,128)S(1)} %bitcast.36), channel_id=1, replica_groups=mesh['z'=4,'y'=4,'core'=2,'tensor'=4] {'tensor'}, dimensions={0}, use_global_device_ids=true | all-gather | bytes 184320 | tf_op jit(solution)/shard_map/all_gather | solution.py:678
  262.8 0.7 reshape.44
  263.4 23.2 %all-to-all-done.5.parcel_ref = bf16[32,328,128]{2,1,0:T(8,128)(2,1)} async-done(((bf16[32,328,128]{2,1,0:T(8,128)(2,1)}), bf16[32,328,128]{2,1,0:T(8,128)(2,1)}, u32[]{:S(2)}, u32[]{:S(2)}) %all-to-all-start.5) | async-done | bytes 2687008 | tf_op jit(solution)/shard_map/all_to_all | solution.py:679
  286.7 4.5 %shard_map.102 = bf16[144,9216]{1,0:T(8,128)(2,1)} custom-call(bf16[32,328,128]{2,1,0:T(8,128)(2,1)} %all-to-all-done.5.parcel_ref), custom_call_target="tpu_custom_call" | custom-call | tf_op jit(solution)/shard_map/pallas_call | solution.py:163
  (60 shorter events, 2.4 us)
Async XLA Ops:
  4.7 10.3 %copy-start.10 = (f32[4,40,256]{2,1,0:T(8,128)}, f32[4,40,256]{2,1,0:T(8,128)S(1)}, u32[]{:S(2)}) copy-start(f32[4,40,256]{2,1,0:T(8,128)S(1)} %pad.8.first) | copy-start | bytes 491524
  4.7 10.9 %collective-permute-start.2 = (f32[4,40,256]{2,1,0:T(8,128)S(1)}, f32[4,40,256]{2,1,0:T(8,128)S(1)}, u32[]{:S(2)}, u32[]{:S(2)}) collective-permute-start(f32[4,40,256]{2,1,0:T(8,128)S(1)} %pad.8.first), channel_id=1, source_target_pairs={{0,1},{1,2},{2,3},{3,0},{4,5},{5,6},{6,7},{7,4},{8,9},{9,10},{10,1... | collective-permute-start | bytes 491528 | tf_op jit(solution)/shard_map/ppermute | solution.py:592
  6.8 9.6 %collective-permute-start.1 = (f32[4,40,256]{2,1,0:T(8,128)S(1)}, f32[4,40,256]{2,1,0:T(8,128)S(1)}, u32[]{:S(2)}, u32[]{:S(2)}) collective-permute-start(f32[4,40,256]{2,1,0:T(8,128)S(1)} %pad.8.first), channel_id=1, source_target_pairs={{0,2},{1,3},{2,0},{3,1},{4,6},{5,7},{6,4},{7,5},{8,10},{9,11},{10,... | collective-permute-start | bytes 491528 | tf_op jit(solution)/shard_map/ppermute | solution.py:592
  9.3 7.1 %collective-permute-start = (f32[4,40,256]{2,1,0:T(8,128)S(1)}, f32[4,40,256]{2,1,0:T(8,128)S(1)}, u32[]{:S(2)}, u32[]{:S(2)}) collective-permute-start(f32[4,40,256]{2,1,0:T(8,128)S(1)} %pad.8.first), channel_id=1, source_target_pairs={{0,3},{1,0},{2,1},{3,2},{4,7},{5,4},{6,5},{7,6},{8,11},{9,8},{10,9... | collective-permute-start | bytes 491528 | tf_op jit(solution)/shard_map/ppermute | solution.py:592
  10.4 4.5 %copy-start.18 = (bf16[144,256]{1,0:T(8,128)(2,1)S(1)}, bf16[144,256]{1,0:T(8,128)(2,1)}, u32[]{:S(2)}) copy-start(bf16[144,256]{1,0:T(8,128)(2,1)} %param.6) | copy-start | bytes 221188
  15.6 0.8 copy-start.15
  16.4 0.6 copy-start.16
  16.4 0.7 copy-start.17
  38.2 9.9 %copy-start.2 = (bf16[16,40,512]{2,1,0:T(8,128)(2,1)}, bf16[16,40,512]{2,1,0:T(8,128)(2,1)S(1)}, u32[]{:S(2)}) copy-start(bf16[16,40,512]{2,1,0:T(8,128)(2,1)S(1)} %all_to_all.30) | copy-start | bytes 1966084
  38.2 41.5 %all-to-all-start.1 = ((bf16[32,328,128]{2,1,0:T(8,128)(2,1)}), bf16[32,328,128]{2,1,0:T(8,128)(2,1)}, u32[]{:S(2)}, u32[]{:S(2)}) async-start(bf16[32,328,128]{2,1,0:T(8,128)(2,1)} %shard_map.92), calls=%async_computation.1 | async-start | bytes 5373952 | tf_op jit(solution)/shard_map/all_to_all | solution.py:651
  45.3 17.3 %collective-permute-start.4 = (bf16[640,512]{1,0:T(8,128)(2,1)S(1)}, bf16[640,512]{1,0:T(8,128)(2,1)S(1)}, u32[]{:S(2)}, u32[]{:S(2)}) collective-permute-start(bf16[640,512]{1,0:T(8,128)(2,1)S(1)} %bitcast.32), channel_id=1, source_target_pairs={{0,1},{1,2},{2,3},{3,0},{4,5},{5,6},{6,7},{7,4},{8,9},{9,10},{10,1... | collective-permute-start | bytes 1966088 | tf_op jit(solution)/shard_map/ppermute | solution.py:601
  46.6 17.5 %collective-permute-start.3 = (bf16[640,512]{1,0:T(8,128)(2,1)S(1)}, bf16[640,512]{1,0:T(8,128)(2,1)S(1)}, u32[]{:S(2)}, u32[]{:S(2)}) collective-permute-start(bf16[640,512]{1,0:T(8,128)(2,1)S(1)} %bitcast.33), channel_id=1, source_target_pairs={{0,3},{1,0},{2,1},{3,2},{4,7},{5,4},{6,5},{7,6},{8,11},{9,8},{10,9... | collective-permute-start | bytes 1966088 | tf_op jit(solution)/shard_map/ppermute | solution.py:601
  48.0 28.9 %collective-permute-start.7 = (bf16[640,512]{1,0:T(8,128)(2,1)S(1)}, bf16[640,512]{1,0:T(8,128)(2,1)S(1)}, u32[]{:S(2)}, u32[]{:S(2)}) collective-permute-start(bf16[640,512]{1,0:T(8,128)(2,1)S(1)} %bitcast.34), channel_id=1, source_target_pairs={{0,4},{4,0},{1,5},{5,1},{2,6},{6,2},{3,7},{7,3},{8,12},{12,8},{9,1... | collective-permute-start | bytes 1966088 | tf_op jit(solution)/shard_map/ppermute | solution.py:597
  62.5 17.1 %copy-start.4 = (bf16[640,512]{1,0:T(8,128)(2,1)}, bf16[640,512]{1,0:T(8,128)(2,1)S(1)}, u32[]{:S(2)}) copy-start(bf16[640,512]{1,0:T(8,128)(2,1)S(1)} %collective-permute-done.4.refs_4_) | copy-start | bytes 1966084
  62.6 9.4 %collective-permute-start.5 = (bf16[320,512]{1,0:T(8,128)(2,1)S(1)}, bf16[320,512]{1,0:T(8,128)(2,1)}, u32[]{:S(2)}, u32[]{:S(2)}) collective-permute-start(bf16[320,512]{1,0:T(8,128)(2,1)S(1)} %slice.12), channel_id=1, source_target_pairs={{0,1},{1,2},{2,3},{3,0},{4,5},{5,6},{6,7},{7,4},{8,9},{9,10},{10,1... | collective-permute-start | bytes 983048 | tf_op jit(solution)/shard_map/ppermute | solution.py:601
  62.7 14.3 %collective-permute-start.11 = (bf16[640,512]{1,0:T(8,128)(2,1)S(1)}, bf16[640,512]{1,0:T(8,128)(2,1)S(1)}, u32[]{:S(2)}, u32[]{:S(2)}) collective-permute-start(bf16[640,512]{1,0:T(8,128)(2,1)S(1)} %collective-permute-done.4.refs_4_), channel_id=1, source_target_pairs={{0,4},{4,0},{1,5},{5,1},{2,6},{6,2},{3,7},{7,3},{8,12},{12,8},{9,1... | collective-permute-start | bytes 1966088 | tf_op jit(solution)/shard_map/ppermute | solution.py:597
  64.1 15.5 %copy-start.5 = (bf16[640,512]{1,0:T(8,128)(2,1)}, bf16[640,512]{1,0:T(8,128)(2,1)S(1)}, u32[]{:S(2)}) copy-start(bf16[640,512]{1,0:T(8,128)(2,1)S(1)} %collective-permute-done.3.refs_1_) | copy-start | bytes 1966084
  64.2 9.9 %collective-permute-start.6 = (bf16[320,512]{1,0:T(8,128)(2,1)S(1)}, bf16[320,512]{1,0:T(8,128)(2,1)}, u32[]{:S(2)}, u32[]{:S(2)}) collective-permute-start(bf16[320,512]{1,0:T(8,128)(2,1)S(1)} %slice.13), channel_id=1, source_target_pairs={{0,3},{1,0},{2,1},{3,2},{4,7},{5,4},{6,5},{7,6},{8,11},{9,8},{10,9... | collective-permute-start | bytes 983048 | tf_op jit(solution)/shard_map/ppermute | solution.py:601
  66.8 10.2 %collective-permute-start.8 = (bf16[640,512]{1,0:T(8,128)(2,1)S(1)}, bf16[640,512]{1,0:T(8,128)(2,1)}, u32[]{:S(2)}, u32[]{:S(2)}) collective-permute-start(bf16[640,512]{1,0:T(8,128)(2,1)S(1)} %collective-permute-done.3.refs_1_), channel_id=1, source_target_pairs={{0,4},{4,0},{1,5},{5,1},{2,6},{6,2},{3,7},{7,3},{8,12},{12,8},{9,1... | collective-permute-start | bytes 1966088 | tf_op jit(solution)/shard_map/ppermute | solution.py:597
  72.0 4.9 %collective-permute-start.9 = (bf16[320,512]{1,0:T(8,128)(2,1)}, bf16[320,512]{1,0:T(8,128)(2,1)}, u32[]{:S(2)}, u32[]{:S(2)}) collective-permute-start(bf16[320,512]{1,0:T(8,128)(2,1)} %collective-permute-done.5.refs_2_), channel_id=1, source_target_pairs={{0,4},{4,0},{1,5},{5,1},{2,6},{6,2},{3,7},{7,3},{8,12},{12,8},{9,1... | collective-permute-start | bytes 983048 | tf_op jit(solution)/shard_map/ppermute | solution.py:597
  74.1 2.9 collective-permute-start.10
  77.0 0.8 copy-start.8
  77.0 2.7 copy-start.9
  89.7 7.7 %copy-start.12 = (f32[256,256]{1,0:T(8,128)S(1)}, f32[256,256]{1,0:T(8,128)}, u32[]{:S(2)}) copy-start(f32[256,256]{1,0:T(8,128)} %get-tuple-element.44.gram_ref) | copy-start | bytes 786436
  94.6 8.1 %collective-permute-start.12 = (bf16[2560,512]{1,0:T(8,128)(2,1)}, bf16[2560,512]{1,0:T(8,128)(2,1)}, u32[]{:S(2)}, u32[]{:S(2)}) collective-permute-start(bf16[2560,512]{1,0:T(8,128)(2,1)} %shard_map.95), channel_id=1, source_target_pairs={{0,4},{4,0},{1,5},{5,1},{2,6},{6,2},{3,7},{7,3},{8,12},{12,8},{9,1... | collective-permute-start | bytes 7864328 | tf_op jit(solution)/shard_map/ppermute | solution.py:597
  97.4 4.8 %collective-permute-start.13 = (f32[256,256]{1,0:T(8,128)S(1)}, f32[256,256]{1,0:T(8,128)S(1)}, u32[]{:S(2)}, u32[]{:S(2)}) collective-permute-start(f32[256,256]{1,0:T(8,128)S(1)} %copy-done.12), channel_id=1, source_target_pairs={{0,4},{4,0},{1,5},{5,1},{2,6},{6,2},{3,7},{7,3},{8,12},{12,8},{9,1... | collective-permute-start | bytes 786440 | tf_op jit(solution)/shard_map/ppermute | solution.py:597
  102.2 0.7 copy-start.13
  180.9 2.4 copy-start
  180.9 27.8 %copy-start.11 = (f32[288,256]{1,0:T(8,128)S(1)}, f32[288,256]{1,0:T(8,128)}, u32[]{:S(2)}) copy-start(f32[288,256]{1,0:T(8,128)} %get-tuple-element.53) | copy-start | bytes 884740
  180.9 5.7 %collective-permute-start.14 = (bf16[2560,256]{1,0:T(8,128)(2,1)S(1)}, bf16[2560,256]{1,0:T(8,128)(2,1)}, u32[]{:S(2)}, u32[]{:S(2)}) collective-permute-start(bf16[2560,256]{1,0:T(8,128)(2,1)S(1)} %bitcast.27), channel_id=1, source_target_pairs={{0,4},{4,0},{1,5},{5,1},{2,6},{6,2},{3,7},{7,3},{8,12},{12,8},{9,1... | collective-permute-start | bytes 3932168 | tf_op jit(solution)/shard_map/ppermute | solution.py:597
  203.7 7.3 %copy-start.3 = (f32[256,256]{1,0:T(8,128)S(1)}, f32[256,256]{1,0:T(8,128)}, u32[]{:S(2)}) copy-start(f32[256,256]{1,0:T(8,128)} %get-tuple-element.49) | copy-start | bytes 786436
  203.7 7.3 %copy-start.6 = (bf16[2560,256]{1,0:T(8,128)(2,1)S(1)}, bf16[2560,256]{1,0:T(8,128)(2,1)}, u32[]{:S(2)}) copy-start(bf16[2560,256]{1,0:T(8,128)(2,1)} %get-tuple-element.51) | copy-start | bytes 3932164
  203.7 24.7 %all-to-all-start.4 = ((bf16[64,40,256]{2,1,0:T(8,128)(2,1)}), bf16[64,40,256]{2,1,0:T(8,128)(2,1)S(1)}, u32[]{:S(2)}, u32[]{:S(2)}) async-start(bf16[64,40,256]{2,1,0:T(8,128)(2,1)} %get-tuple-element.50), calls=%async_computation.4 | async-start | bytes 2621440 | tf_op jit(solution)/shard_map/all_to_all | solution.py:612
  208.7 4.5 %copy-start.7 = (bf16[2560,256]{1,0:T(8,128)(2,1)S(1)}, bf16[2560,256]{1,0:T(8,128)(2,1)}, u32[]{:S(2)}) copy-start(bf16[2560,256]{1,0:T(8,128)(2,1)} %get-tuple-element.52) | copy-start | bytes 3932164
  211.0 20.2 %copy-start.19 = (f32[1,256]{1,0:T(1,128)S(1)}, f32[1,256]{1,0:T(1,128)}, u32[]{:S(2)}) copy-start(f32[1,256]{1,0:T(1,128)} %get-tuple-element.61) | copy-start | bytes 3076
  211.0 20.7 %copy-start.14 = (f32[40,512]{1,0:T(8,128)S(1)}, f32[40,512]{1,0:T(8,128)}, u32[]{:S(2)}) copy-start(f32[40,512]{1,0:T(8,128)} %get-tuple-element.45.sums_ref) | copy-start | bytes 245764
  228.4 3.7 %copy-start.1 = (bf16[64,40,256]{2,1,0:T(8,128)(2,1)}, bf16[64,40,256]{2,1,0:T(8,128)(2,1)S(1)}, u32[]{:S(2)}) copy-start(bf16[64,40,256]{2,1,0:T(8,128)(2,1)S(1)} %all-to-all-done.4) | copy-start | bytes 3932164
  228.4 8.8 %collective-permute-start.15 = (bf16[2560,256]{1,0:T(8,128)(2,1)S(1)}, bf16[2560,256]{1,0:T(8,128)(2,1)}, u32[]{:S(2)}, u32[]{:S(2)}) collective-permute-start(bf16[2560,256]{1,0:T(8,128)(2,1)S(1)} %bitcast.29), channel_id=1, source_target_pairs={{0,4},{4,0},{1,5},{5,1},{2,6},{6,2},{3,7},{7,3},{8,12},{12,8},{9,1... | collective-permute-start | bytes 3932168 | tf_op jit(solution)/shard_map/ppermute | solution.py:597
  247.8 38.9 %all-to-all-start.5 = ((bf16[32,328,128]{2,1,0:T(8,128)(2,1)}), bf16[32,328,128]{2,1,0:T(8,128)(2,1)}, u32[]{:S(2)}, u32[]{:S(2)}) async-start(bf16[32,328,128]{2,1,0:T(8,128)(2,1)} %bitcast.25), calls=%async_computation.5 | async-start | bytes 5373952 | tf_op jit(solution)/shard_map/all_to_all | solution.py:679
